TPU v7x, 512 devices: a whole 4x8x8 slice. The times are simulated.
512 devices in a mesh: leaf: 4 (over y_hi, core), row: 4 (over x), col: 32 (over y_lo, z).
Axes of the slice: x: 4, y: 8 (y_hi: 2, y_lo: 4; y = y_hi * 4 + y_lo), z: 8, core: 2. Of those that a mesh axis runs over, the one named last changes fastest.
Arguments:
- root_inverse: bfloat16 [4096, 4096], P('col', ('leaf', 'row')), as said below
- factor_first: bfloat16 [2, 4096, 2048], P(None, 'col', 'row'), may hold values from -0.09375 to 0.09375
- local_first: bfloat16 [2, 2048, 2048], P(None, 'col', 'row'), as said below
- factor_second: bfloat16 [4, 4096, 1536], P('leaf', 'col', 'row'), may hold values from -0.09375 to 0.09375
- local_second: float32 [4, 1536], P('leaf', 'row'), may hold values from 0.5 to 2
- ancestor_map: int32 [4, 16], replicated, may hold values from 0 to 31, as said below
Outputs:
- variance: float32 [4, 1536], P('leaf', 'row')
Inputs may be any that keep to these rules, and one draw needn't show every extreme that they name: `ancestor_map`: each row lists 16 different root blocks; some row names block 0 and some row names block 31. `root_inverse`: Symmetric. `local_first`: symmetric in its last two dimensions.
All inputs are finite; a program needn't handle non-finite values.
Results may differ from a plain program's by a relative error of at most 0.0003.
Values may be sent and summed in bfloat16 or wider, within the bound.
A program may use at most 64 MiB of HBM per device.

v0:
```python
import jax
import jax.numpy as jnp
from jax import lax
from jax.sharding import PartitionSpec as P

BLK = 128
NBR = 32
K2 = 16
R = 4096
ANC2 = 2048


def local(root_inverse, factor_first, local_first, factor_second, local_second, ancestor_map):
    highest = lax.Precision.HIGHEST
    subtree = lax.axis_index("leaf")
    parent = subtree // 2
    column = lax.axis_index("col")
    root_rows = lax.all_gather(root_inverse, ("leaf", "row"), axis=1, tiled=True)
    own_factor = lax.dynamic_index_in_dim(factor_first, parent, 0, keepdims=False)
    own_local = lax.dynamic_index_in_dim(local_first, parent, 0, keepdims=False)
    factor_rows = lax.all_gather(own_factor, "row", axis=1, tiled=True)
    row_count = root_inverse.shape[0]
    gathered = lax.all_gather(factor_second[0], "col", axis=0, tiled=True)
    root_part = gathered[:ANC2]
    parent_part = gathered[ANC2:].astype(jnp.float32)
    slot_ids = lax.dynamic_index_in_dim(ancestor_map, subtree, 0, keepdims=False)
    positions = column * row_count + jnp.arange(row_count, dtype=jnp.int32)
    matches = (positions // BLK)[:, None] == slot_ids[None, :]
    present = jnp.any(matches, 1)
    slot_of = jnp.sum(jnp.where(matches, jnp.arange(K2, dtype=jnp.int32)[None, :], 0), 1)
    picked = jnp.take(root_part, slot_of * BLK + positions % BLK, axis=0)
    own_padded = jnp.where(present[:, None], picked, jnp.zeros_like(picked))
    cross_block = jnp.dot(
        root_rows,
        lax.all_gather(own_factor, "col", axis=0, tiled=True),
        preferred_element_type=jnp.float32,
    )
    factor_block = factor_rows.astype(jnp.float32)
    summed = lax.psum_scatter(
        jnp.dot(factor_block.T, cross_block, precision=highest).astype(jnp.bfloat16),
        "col",
        scatter_dimension=0,
        tiled=True,
    ).astype(jnp.float32)
    parent_inv = own_local.astype(jnp.float32) + summed
    cross_rows, parent_rows = (
        lax.all_gather(cross_block.astype(jnp.bfloat16), "row", axis=1, tiled=True).astype(
            cross_block.dtype
        ),
        lax.all_gather(parent_inv.astype(jnp.bfloat16), "row", axis=1, tiled=True).astype(
            parent_inv.dtype
        ),
    )
    chooser = (jnp.arange(NBR, dtype=jnp.int32)[:, None] == slot_ids[None, :]).astype(jnp.bfloat16)
    blocks = root_part.reshape(K2, BLK, root_part.shape[1])
    padded = (
        jnp.einsum("ek,kbt->ebt", chooser, blocks, preferred_element_type=jnp.float32)
        .astype(jnp.bfloat16)
        .reshape(R, root_part.shape[1])
    )
    root_term = jnp.dot(root_rows, padded, preferred_element_type=jnp.float32)
    cross_term = jnp.dot(cross_rows, parent_part, precision=highest)
    parent_term = jnp.dot(parent_rows, parent_part, precision=highest)
    parent_count = parent_rows.shape[0]
    own_lower = lax.dynamic_slice_in_dim(parent_part, column * parent_count, parent_count, 0)
    partial_value = jnp.sum(
        own_padded.astype(jnp.float32) * (root_term - 2.0 * cross_term), 0
    ) + jnp.sum(own_lower * parent_term, 0)
    summed_var = lax.psum(partial_value, "col")
    return local_second + summed_var[None, :]


def solution(mesh):
    placed = (
        P("col", ("leaf", "row")),
        P(None, "col", "row"),
        P(None, "col", "row"),
        P("leaf", "col", "row"),
        P("leaf", "row"),
        P(),
    )
    return jax.shard_map(
        local, mesh=mesh, in_specs=placed, out_specs=P("leaf", "row"), check_vma=False
    )
```

profile of v0, /device:TPU:2, one launch (start us, length us, event | category | flops | bytes accessed | tf_op | source)
XLA Modules:
  0.0 649.7 jit_solution(167872410792754334)
XLA Ops:
  6.5 0.7 all-gather.7.cloned.1.call-update
  7.3 0.0 all-gather.11.cloned.1.call-start
  7.3 0.2 copy-done
  7.5 0.7 constant_dynamic-slice_fusion
  8.2 0.0 all-gather.9.cloned.1.call-start
  8.2 0.7 all-gather.9.cloned.1.call-update
  8.9 0.0 reduce-scatter.2.cloned.1.call-start
  9.0 15.7 %all-gather.2 = bf16[1,128,2048]{2,1,0:T(8,128)(2,1)S(1)} all-gather(bf16[1,128,512]{2,1,0:T(8,128)(2,1)} %constant_dynamic-slice_fusion), channel_id=4, replica_groups=mesh['leaf'=4,'row'=4,'col'=32] {'row'}, dimensions={2}, use_global_device_ids=true | all-gather | bytes 655360 | tf_op jit(solution)/shard_map/all_gather | solution.py:21
  24.7 48.8 %all-gather.7.cloned.1.call-done = bf16[128,4096]{1,0:T(8,128)(2,1)} async-done(((bf16[128,256]{1,0:T(8,128)(2,1)}), bf16[128,4096]{1,0:T(8,128)(2,1)}) %all-gather.7.cloned.1.call-update) | async-done | bytes 1048592 | tf_op jit(solution)/shard_map/all_gather | solution.py:18
  73.5 161.3 %all-gather.11.cloned.1.call-done = bf16[1,4096,512]{2,1,0:T(8,128)(2,1)} async-done(((bf16[1,128,512]{2,1,0:T(8,128)(2,1)}), bf16[1,4096,512]{2,1,0:T(8,128)(2,1)}) %all-gather.11.cloned.1.call-update) | async-done | bytes 4194320 | tf_op jit(solution)/shard_map/all_gather | solution.py:35
  234.8 3.8 fusion
  238.6 0.7 copy-done.2
  239.3 3.2 convolution_convert_fusion
  242.5 0.0 reduce-scatter.2.cloned.1.call-update
  242.6 0.7 fusion.15
  243.2 0.1 fusion.9
  243.4 0.1 compare_reduce_fusion
  243.5 146.1 %all-gather.9.cloned.1.call-done = bf16[1,4096,384]{2,1,0:T(8,128)(2,1)} async-done(((bf16[1,128,384]{2,1,0:T(8,128)(2,1)}), bf16[1,4096,384]{2,1,0:T(8,128)(2,1)}) %all-gather.9.cloned.1.call-update) | async-done | bytes 3145744 | tf_op jit(solution)/shard_map/all_gather | solution.py:23
  389.5 4.0 slice_bitcast_fusion
  393.5 1.3 convolution_convert_fusion.1
  394.8 1.1 copy.10
  396.0 2.5 gather_fusion
  398.4 1.1 convert_bitcast_fusion
  399.5 12.8 %all_gather.21 = bf16[128,2048]{0,1:T(8,128)(2,1)S(1)} all-gather(bf16[128,512]{0,1:T(8,128)(2,1)S(1)} %convert_bitcast_fusion), channel_id=1, replica_groups=mesh['leaf'=4,'row'=4,'col'=32] {'row'}, dimensions={1}, use_global_device_ids=true | all-gather | bytes 655360 | tf_op jit(solution)/shard_map/all_gather | solution.py:47
  412.3 1.9 convolution_multiply_fusion
  414.2 0.7 fusion.5
  414.9 137.1 %reduce-scatter.2.cloned.1.call-done = bf16[64,512]{1,0:T(8,128)(2,1)} async-done(((bf16[2048,512]{1,0:T(8,128)(2,1)}), bf16[64,512]{1,0:T(8,128)(2,1)}) %reduce-scatter.2.cloned.1.call-update) | async-done | bytes 65552 | tf_op jit(solution)/shard_map/reduce_scatter | solution.py:39
  552.0 0.9 fusion.8
  552.9 12.3 %all_gather.23 = bf16[64,2048]{1,0:T(8,128)(2,1)S(1)} all-gather(bf16[64,512]{1,0:T(8,128)(2,1)S(1)} %fusion.8), channel_id=1, replica_groups=mesh['leaf'=4,'row'=4,'col'=32] {'row'}, dimensions={1}, use_global_device_ids=true | all-gather | bytes 327680 | tf_op jit(solution)/shard_map/all_gather | solution.py:50
  565.2 1.8 fusion.6
  567.0 75.6 %psum.7 = f32[1,384]{1,0:T(1,128)S(1)} all-reduce(f32[1,384]{1,0:T(1,128)S(1)} %broadcast_in_dim.48), channel_id=1, replica_groups=mesh['leaf'=4,'row'=4,'col'=32] {'col'}, use_global_device_ids=true, to_apply=%region_5.6 | all-reduce | flops 384 | bytes 3072 | tf_op jit(solution)/shard_map/psum | solution.py:69
  642.6 0.6 add.123
  (14 shorter events, 0.1 us)
Async XLA Ops:
  6.5 1.0 copy-start
  6.5 67.0 %all-gather.7.cloned.1.call-start = ((), (), s32[]{:S(2)}) async-start(), calls=%async_computation.1 | async-start | bytes 1114112 | tf_op jit(solution)/shard_map/all_gather | solution.py:18
  7.3 227.6 %all-gather.11.cloned.1.call-start = ((), (), s32[]{:S(2)}) async-start(), calls=%async_computation.4 | async-start | bytes 4325376 | tf_op jit(solution)/shard_map/all_gather | solution.py:35
  8.2 381.4 %all-gather.9.cloned.1.call-start = ((), (), s32[]{:S(2)}) async-start(), calls=%async_computation.3 | async-start | bytes 3244032 | tf_op jit(solution)/shard_map/all_gather | solution.py:23
  8.9 543.1 %reduce-scatter.2.cloned.1.call-start = ((), (), s32[]{:S(2)}) async-start(), calls=%async_computation.2 | async-start | bytes 2162688 | tf_op jit(solution)/shard_map/reduce_scatter | solution.py:39
  238.6 0.7 copy-start.2
  398.4 15.8 %copy-start.1 = (bf16[128,4096]{1,0:T(8,128)(2,1)S(1)}, bf16[128,4096]{1,0:T(8,128)(2,1)}, u32[]{:S(2)}) copy-start(bf16[128,4096]{1,0:T(8,128)(2,1)} %all-gather.7.cloned.1.call-done) | copy-start | bytes 3145732
  414.9 227.7 %copy-start.3 = (f32[1,384]{1,0:T(1,128)S(1)}, f32[1,384]{1,0:T(1,128)}, u32[]{:S(2)}) copy-start(f32[1,384]{1,0:T(1,128)} %param.10) | copy-start | bytes 4612
Sparse Core Ops, SparseCore 0:
  10.5 62.9 all-gather.6
  75.6 159.1 all-gather.10
  236.9 152.5 all-gather.8
  392.2 159.7 reduce-scatter.1
where the time goes:
time: 650 us
  waiting for transfers between devices  495 us (76%)
  blocking collectives  116 us (18%)
  between operations  13.2 us (2%)
  matrix products  12.7 us (2%)
  local copies, waits for them, and re-layouts  9.82 us (2%)
    all_gather x1, waiting for transfers between devices, local(): lax.all_gather(own_factor, 'col', axis=0, tiled=True)  161 us
    all_gather x1, waiting for transfers between devices, local(): gathered = lax.all_gather(factor_second[0], 'col', axis=0, tiled=True)  146 us
    reduce_scatter x1, waiting for transfers between devices, local(): lax.psum_scatter(jnp.dot(factor_block.T, cross_block, precision=highest)....  137 us
    psum x1, blocking collectives, local(): summed_var = lax.psum(partial_value, 'col')  75.6 us
    all_gather x1, waiting for transfers between devices, local(): lax.all_gather(root_inverse, ('leaf', 'row'), axis=1, tiled=True)  48.8 us
    all_gather x1, blocking collectives, local(): factor_rows = lax.all_gather(own_factor, 'row', axis=1, tiled=True)  15.7 us
  transfers between devices with their start and end apart: 4, of which 4 were waited for; matrix products, arithmetic and copies ran while one was open for 3% of the time, Pallas kernels for 0%

commit v1 on v0

v1 whole, which is shorter than its diff:
```python
import jax
import jax.numpy as jnp
from jax import lax
from jax.experimental import pallas as pl
from jax.experimental.pallas import tpu as pltpu
from jax.sharding import PartitionSpec as P

NX, NU, NZ = 4, 4, 8
BLK = 128
SUB = 96
SLOTS = 16
MESH = pl.DeviceIdType.MESH
BF16, F32 = jnp.bfloat16, jnp.float32
NT = (((1,), (1,)), ((), ()))


def dot_nt(a, b):
    return lax.dot_general(a, b, NT, preferred_element_type=F32)


def kernel(
    r_ref, f_ref, l_ref, v_ref, loc_ref, map_ref, out_ref,
    vs, vall, fg, lg, rg, wk, wm, acc, sums, red1, red2,
    own_sem, vsc_s, vsc_r, vz_s, vz_r, fy_s, fy_r, fx_s, fx_r, fd_s, fd_r,
    ly_s, ly_r, lx_s, lx_r, ld_s, ld_r, ry_s, ry_r, rx_s, rx_r, rd_s, rd_r,
    wc_s, wc_r, wf_s, wf_r, wz_s, wz_r, d1_s, d1_r, d2_s, d2_r,
):
    leaf, x, col = lax.axis_index("leaf"), lax.axis_index("row"), lax.axis_index("col")
    h, c = lax.div(leaf, 2), lax.rem(leaf, 2)
    u, z = lax.div(col, NZ), lax.rem(col, NZ)
    y = h * NU + u
    sgn = 1 - 2 * c

    def at_z(zz):
        return (leaf, x, u * NZ + zz)

    def at_u(uu):
        return (leaf, x, uu * NZ + z)

    def at_x(xx):
        return (leaf, xx, col)

    def at_y(yy, core):
        return (lax.div(yy, NU) * 2 + core, x, lax.rem(yy, NU) * NZ + z)

    def zmod(v):
        return lax.rem(v + 2 * NZ, NZ)

    def xmod(v):
        return lax.rem(v + 2 * NX, NX)

    def umod(v):
        return lax.rem(v + 2 * NU, NU)

    started = []

    def send(src, dst, ssem, rsem, to):
        copy = pltpu.make_async_remote_copy(
            src_ref=src, dst_ref=dst, send_sem=ssem, recv_sem=rsem, device_id=to, device_id_type=MESH
        )
        copy.start()
        started.append(copy)

    def arrived(dst, rsem):
        pltpu.make_async_remote_copy(
            src_ref=dst, dst_ref=dst, send_sem=rsem, recv_sem=rsem, device_id=at_z(zmod(z + 1)), device_id_type=MESH
        ).wait_recv()

    barrier = pltpu.get_barrier_semaphore()
    peers = []
    for d in range(1, 16):
        number = lax.rem(y * 2 + c + d, 16)
        peers.append(at_y(lax.div(number, 2), lax.rem(number, 2)))
    peers += [at_z(zmod(z + d)) for d in range(1, NZ)]
    peers += [at_x(xmod(x + 1)), at_x(xmod(x - 1))]
    for peer in peers:
        pl.semaphore_signal(barrier, inc=1, device_id=peer, device_id_type=MESH)

    half = pl.ds(pl.multiple_of(c * 64, 64), 64)
    quarter = pl.ds(pl.multiple_of(c * 32, 32), 32)
    own_f = pltpu.make_async_copy(f_ref.at[h, half], fg.at[x, u, c], own_sem.at[0])
    own_l = pltpu.make_async_copy(l_ref.at[h, quarter], lg.at[x, u, c], own_sem.at[1])
    own_f.start()
    own_l.start()
    vt = jnp.transpose(v_ref[0].astype(F32)).astype(BF16)
    vs[...] = vt.reshape(NU, SUB, BLK)
    vall[z, u] = vs[u]
    own_f.wait()
    own_l.wait()
    pl.semaphore_wait(barrier, len(peers))

    for d in range(1, NU):
        to = umod(u + d)
        send(vs.at[to], vall.at[z, u], vsc_s.at[d], vsc_r.at[d], at_u(to))
    xa, xb = xmod(x + sgn), xmod(x - sgn)
    y_steps = [sgn, -sgn, 2 * sgn]
    for i, step in enumerate(y_steps):
        yy = lax.rem(y + step + 16, 8)
        send(f_ref.at[lax.div(yy, NU), half], fg.at[x, u, c], fy_s.at[i], fy_r.at[i], at_y(yy, c))
    u_from = [u] + [umod(u - step) for step in y_steps]

    def f_x_first(i):
        send(fg.at[x, u_from[i], c], fg.at[x, u_from[i], c], fx_s.at[i, 0], fx_r.at[i, 0], at_x(xa))
        send(fg.at[x, u_from[i], c], fg.at[x, u_from[i], c], fx_s.at[i, 1], fx_r.at[i, 1], at_x(xb))

    def f_x_second(i):
        arrived(fg.at[xb, u_from[i], c], fx_r.at[i, 0])
        send(fg.at[xb, u_from[i], c], fg.at[xb, u_from[i], c], fx_s.at[i, 2], fx_r.at[i, 2], at_x(xa))

    f_x_first(0)
    target = leaf
    for t in range(2):
        for core in range(2):
            rows = r_ref.at[pl.ds(core * 64, 64)]
            place = rg.at[x, u, core]
            mine = jnp.logical_and(jnp.logical_and(h == t, c == core), u == target)

            @pl.when(mine)
            def _():
                pltpu.make_async_copy(rows, place, ry_r.at[u]).start()

            @pl.when(jnp.logical_not(mine))
            def _():
                pltpu.make_async_remote_copy(
                    src_ref=rows, dst_ref=place, send_sem=ry_s.at[t * 2 + core], recv_sem=ry_r.at[u],
                    device_id=(2 * t + core, x, target * NZ + z), device_id_type=MESH,
                ).start()
    for i, step in enumerate(y_steps):
        yy = lax.rem(y + step + 16, 8)
        send(l_ref.at[lax.div(yy, NU), quarter], lg.at[x, u, c], ly_s.at[i], ly_r.at[i], at_y(yy, c))

    za, zb = zmod(z + sgn), zmod(z - sgn)
    for d in range(1, NU):
        arrived(vall.at[z, umod(u - d)], vsc_r.at[d])

    def ring_z(array, part, ssem, rsem, forward, s):
        origin = zmod(z - sgn * (s - 1)) if forward else zmod(z + sgn * (s - 1))
        block = array.at[origin] if part is None else array.at[origin, part]
        if s > 1:
            arrived(block, rsem.at[s - 1])
        send(block, block, ssem.at[s], rsem.at[s], at_z(za if forward else zb))

    def ring_z_last(array, part, rsem, forward, s):
        origin = zmod(z - sgn * s) if forward else zmod(z + sgn * s)
        arrived(array.at[origin] if part is None else array.at[origin, part], rsem.at[s])

    low, high = pl.ds(0, 2), pl.ds(2, 2)
    rings = [(high, 0, True, 4), (high, 1, False, 3), (low, 2, True, 3), (low, 3, False, 4)]

    def v_step(s):
        for part, number, forward, last in rings:
            if s <= last:
                ring_z(vall, part, vz_s.at[number], vz_r.at[number], forward, s)

    v_step(1)
    for i in range(1, 4):
        arrived(fg.at[x, u_from[i], c], fy_r.at[i - 1])
        f_x_first(i)

    sibling = (h * 2 + 1 - c, x, col)

    def to_sibling(array, xx, i, ssem, rsem):
        send(array.at[xx, :, c], array.at[xx, :, c], ssem.at[i], rsem.at[i], sibling)

    x_from = [x, xb, xa, xmod(x - 2 * sgn)]
    to_sibling(fg, x, 0, fd_s, fd_r)
    v_step(2)
    f_x_second(0)
    f_x_second(1)
    v_step(3)
    f_x_second(2)
    f_x_second(3)
    to_sibling(fg, xb, 1, fd_s, fd_r)
    v_step(4)
    for i in range(4):
        arrived(fg.at[xa, u_from[i], c], fx_r.at[i, 1])
    to_sibling(fg, xa, 2, fd_s, fd_r)
    for i in range(4):
        arrived(rg.at[x, i, c], ry_r.at[i])

    def bulk_x_first(array, ssem, rsem):
        send(array.at[x, :, c], array.at[x, :, c], ssem.at[0], rsem.at[0], at_x(xa))
        send(array.at[x, :, c], array.at[x, :, c], ssem.at[1], rsem.at[1], at_x(xb))

    def bulk_x_second(array, ssem, rsem):
        arrived(array.at[xb, :, c], rsem.at[0])
        send(array.at[xb, :, c], array.at[xb, :, c], ssem.at[2], rsem.at[2], at_x(xa))

    bulk_x_first(rg, rx_s, rx_r)
    for i in range(4):
        arrived(fg.at[xmod(x - 2 * sgn), u_from[i], c], fx_r.at[i, 2])
    to_sibling(fg, x_from[3], 3, fd_s, fd_r)
    for i in range(1, 4):
        arrived(lg.at[x, u_from[i], c], ly_r.at[i - 1])
    bulk_x_first(lg, lx_s, lx_r)
    to_sibling(rg, x, 0, rd_s, rd_r)
    to_sibling(lg, x, 0, ld_s, ld_r)

    ring_z_last(vall, high, vz_r.at[0], True, 4)
    ring_z_last(vall, high, vz_r.at[1], False, 3)
    for i in range(4):
        xx = [x, xa, xb, xmod(x + 2 * sgn)][i]
        arrived(fg.at[xx, :, 1 - c], fd_r.at[i])

    def p_chunk(xx):
        return jnp.concatenate([vall[4 * (xx % 2) + i, 2 + xx // 2] for i in range(4)], axis=1)

    for pair in range(2):
        total = jnp.zeros((SUB, 256), F32)
        for xx in range(NX):
            total += dot_nt(p_chunk(xx), fg[xx, 2 * pair:2 * pair + 2].reshape(256, 512))
        acc[pair] = total
    ring_z_last(vall, low, vz_r.at[2], True, 3)
    ring_z_last(vall, low, vz_r.at[3], False, 4)
    for b in range(NU):
        block = b * NZ + z
        slot = jnp.int32(0)
        present = jnp.int32(0)
        for k in range(SLOTS):
            hit = map_ref[leaf, k] == block
            slot = jnp.where(hit, k, slot)
            present = jnp.where(hit, 1, present)
        padded = vall[lax.rem(slot, NZ), lax.div(slot, NZ)].astype(F32) * present.astype(F32)
        wm[u, b] = (padded - acc[b // 2, :, (b % 2) * BLK:(b % 2 + 1) * BLK]).astype(BF16)
    wk[z, u] = wm[u, u]

    for d in range(1, NU):
        to = umod(u + d)
        send(wm.at[u, to], wk.at[z, u], wc_s.at[d], wc_r.at[d], at_u(to))
    for d in range(1, NU):
        arrived(wk.at[z, umod(u - d)], wc_r.at[d])

    def w_step(s):
        ring_z(wk, None, wz_s.at[0], wz_r.at[0], True, s)
        if s <= 3:
            ring_z(wk, None, wz_s.at[1], wz_r.at[1], False, s)

    w_step(1)
    for d in range(1, NU):
        to = umod(u + d)
        send(wm.at[u], wm.at[u], wf_s.at[d], wf_r.at[d], at_u(to))
    bulk_x_second(rg, rx_s, rx_r)
    bulk_x_second(lg, lx_s, lx_r)
    w_step(2)
    for array, ssem, rsem, xsem in ((rg, rd_s, rd_r, rx_r), (lg, ld_s, ld_r, lx_r)):
        to_sibling(array, xb, 1, ssem, rsem)
        arrived(array.at[xa, :, c], xsem.at[1])
        to_sibling(array, xa, 2, ssem, rsem)
    w_step(3)
    for array, ssem, rsem, xsem in ((rg, rd_s, rd_r, rx_r), (lg, ld_s, ld_r, lx_r)):
        arrived(array.at[x_from[3], :, c], xsem.at[2])
        to_sibling(array, x_from[3], 3, ssem, rsem)
    w_step(4)
    for i in range(4):
        xx = [x, xa, xb, xmod(x + 2 * sgn)][i]
        arrived(lg.at[xx, :, 1 - c], ld_r.at[i])

    total = jnp.zeros((SUB, 256), F32)
    for xx in range(NX):
        total += dot_nt(p_chunk(xx), lg[xx].reshape(256, 512))
    lane = lax.broadcasted_iota(jnp.int32, (SUB, BLK), 1)
    odd = lax.rem(z, 2).astype(F32)
    l_sum = jnp.zeros((SUB, BLK), F32)
    for pair in range(2):
        first, second = (vall[4 * i + lax.div(z, 2), 2 + pair].astype(F32) for i in range(2))
        first_turned, second_turned = pltpu.roll(first, 64, 1), pltpu.roll(second, 64, 1)
        rows = jnp.where(
            lane < 64,
            first_turned * odd + first * (1.0 - odd),
            second * odd + second_turned * (1.0 - odd),
        )
        l_sum += rows * total[:, pair * BLK:(pair + 1) * BLK]

    for i in range(4):
        xx = [x, xa, xb, xmod(x + 2 * sgn)][i]
        arrived(rg.at[xx, :, 1 - c], rd_r.at[i])
    for d in range(1, NU):
        arrived(wm.at[umod(u - d)], wf_r.at[d])
    ring_z_last(wk, None, wz_r.at[1], False, 3)
    ring_z_last(wk, None, wz_r.at[0], True, 4)

    left = jnp.concatenate([wk[i].reshape(NU * SUB, BLK) for i in range(NZ)], axis=1)
    part = jnp.zeros((NU * SUB, BLK), F32)
    for pair in range(2):
        right = jnp.concatenate([rg[xx, 2 * pair:2 * pair + 2].reshape(256, 256) for xx in range(NX)], axis=1)
        term = dot_nt(left, right)
        for i in range(2):
            rows = wm[:, 2 * pair + i].reshape(NU * SUB, BLK).astype(F32)
            part += rows * term[:, i * BLK:(i + 1) * BLK]
    sums[...] = part
    own_rows = pl.ds(pl.multiple_of(u * SUB, SUB), SUB)
    sums[own_rows, :] = sums[own_rows, :] + l_sum
    flat = jnp.sum(jnp.transpose(sums[...]), axis=0, keepdims=True)
    red1[z] = jnp.concatenate(
        [flat[:, i * BLK:(i + 1) * BLK] for i in range(3)] + [jnp.zeros((5, BLK), F32)], axis=0
    )
    for d in range(1, NZ):
        send(red1.at[z], red1.at[z], d1_s.at[d], d1_r.at[d], at_z(zmod(z + d)))
    for d in range(1, NZ):
        arrived(red1.at[zmod(z - d)], d1_r.at[d])
    red2[u] = jnp.sum(red1[...], axis=0)
    for d in range(1, NU):
        send(red2.at[u], red2.at[u], d2_s.at[d], d2_r.at[d], at_u(umod(u + d)))
    for d in range(1, NU):
        arrived(red2.at[umod(u - d)], d2_r.at[d])
    result = jnp.sum(red2[...], axis=0)
    out_ref[...] = loc_ref[...] + jnp.concatenate([result[i:i + 1] for i in range(3)], axis=1)

    for copy in started:
        copy.wait_send()
    for t in range(2):
        for core in range(2):
            mine = jnp.logical_and(jnp.logical_and(h == t, c == core), u == target)

            @pl.when(jnp.logical_not(mine))
            def _():
                pltpu.make_async_remote_copy(
                    src_ref=r_ref.at[pl.ds(core * 64, 64)], dst_ref=rg.at[x, u, core],
                    send_sem=ry_s.at[t * 2 + core], recv_sem=ry_r.at[u],
                    device_id=(2 * t + core, x, target * NZ + z), device_id_type=MESH,
                ).wait_send()


def local(root_inverse, factor_first, local_first, factor_second, local_second, ancestor_map):
    vmem = pl.BlockSpec(memory_space=pltpu.VMEM)
    dma = pltpu.SemaphoreType.DMA
    scratch = [
        pltpu.VMEM((NU, SUB, BLK), BF16),
        pltpu.VMEM((NZ, NU, SUB, BLK), BF16),
        pltpu.VMEM((NX, NU, 2, 64, 512), BF16),
        pltpu.VMEM((NX, NU, 2, 32, 512), BF16),
        pltpu.VMEM((NX, NU, 2, 64, 256), BF16),
        pltpu.VMEM((NZ, NU, SUB, BLK), BF16),
        pltpu.VMEM((NU, NU, SUB, BLK), BF16),
        pltpu.VMEM((2, SUB, 256), F32),
        pltpu.VMEM((NU * SUB, BLK), F32),
        pltpu.VMEM((NZ, 8, BLK), F32),
        pltpu.VMEM((NU, 8, BLK), F32),
        dma((2,)),
    ]
    for count in ((4,), (4, 5), (3,), (4, 3), (4,), (3,), (3,), (4,), (4,), (3,), (4,), (4,), (4,), (2, 5), (8,), (4,)):
        scratch += [dma(count), dma(count)]
    return pl.pallas_call(
        kernel,
        out_shape=jax.ShapeDtypeStruct(local_second.shape, F32),
        in_specs=[vmem, vmem, vmem, vmem, vmem, pl.BlockSpec(memory_space=pltpu.SMEM)],
        out_specs=vmem,
        scratch_shapes=scratch,
        compiler_params=pltpu.CompilerParams(
            collective_id=0, has_side_effects=True, vmem_limit_bytes=32 * 1024 * 1024
        ),
        name="variances",
    )(root_inverse, factor_first, local_first, factor_second, local_second, ancestor_map)


def solution(mesh):
    placed = (
        P("col", ("leaf", "row")),
        P(None, "col", "row"),
        P(None, "col", "row"),
        P("leaf", "col", "row"),
        P("leaf", "row"),
        P(),
    )
    return jax.shard_map(
        local, mesh=mesh, in_specs=placed, out_specs=P("leaf", "row"), check_vma=False
    )
```

time: 650 us -> 73 us (0.11)
  the two profiles are of different devices: /device:TPU:2 before, /device:TPU:56 now
where the time goes in v1:
time: 73 us; the launch traced here: 72.7 us
  Pallas kernels  67.2 us (92%)
  local copies, waits for them, and re-layouts  5.51 us (8%)
    pallas_call x1, Pallas kernels, local(): pl.pallas_call(kernel, out_shape=jax.ShapeDtypeStruct(local_second.shape,...  67.2 us
    unnamed x13, local copies, waits for them, and re-layouts  5.51 us

profile of v1, /device:TPU:56, one launch (start us, length us, event | category | flops | bytes accessed | tf_op | source)
XLA Modules:
  0.0 72.7 jit_solution(4461890029219424287)
XLA Ops:
  0.0 0.0 copy-start
  0.0 0.9 %copy-done = bf16[2,128,512]{2,1,0:T(8,128)(2,1)S(1)} copy-done((bf16[2,128,512]{2,1,0:T(8,128)(2,1)S(1)}, bf16[2,128,512]{2,1,0:T(8,128)(2,1)}, u32[]{:S(2)}) %copy-start) | copy-done | bytes 262168
  1.0 0.0 copy-start.1
  1.0 0.9 %copy-done.1 = bf16[2,64,512]{2,1,0:T(8,128)(2,1)S(1)} copy-done((bf16[2,64,512]{2,1,0:T(8,128)(2,1)S(1)}, bf16[2,64,512]{2,1,0:T(8,128)(2,1)}, u32[]{:S(2)}) %copy-start.1) | copy-done | bytes 131096
  1.9 0.0 copy-start.2
  1.9 0.9 %copy-done.2 = bf16[1,128,384]{2,1,0:T(8,128)(2,1)S(1)} copy-done((bf16[1,128,384]{2,1,0:T(8,128)(2,1)S(1)}, bf16[1,128,384]{2,1,0:T(8,128)(2,1)}, u32[]{:S(2)}) %copy-start.2) | copy-done | bytes 98328
  2.7 0.0 copy-start.3
  2.8 0.8 %copy-done.3 = bf16[128,256]{1,0:T(8,128)(2,1)S(1)} copy-done((bf16[128,256]{1,0:T(8,128)(2,1)S(1)}, bf16[128,256]{1,0:T(8,128)(2,1)}, u32[]{:S(2)}) %copy-start.3) | copy-done | bytes 65560
  3.6 0.0 copy-start.4
  3.6 0.7 copy-done.4
  4.3 0.0 copy-start.5
  4.3 0.7 copy-done.5
  5.0 67.2 %variances.1 = f32[1,384]{1,0:T(1,128)S(1)} custom-call(bf16[128,256]{1,0:T(8,128)(2,1)S(1)} %copy-done.3, bf16[2,128,512]{2,1,0:T(8,128)(2,1)S(1)} %copy-done, bf16[2,64,512]{2,1,0:T(8,128)(2,1)S(1)} %copy-done.1, bf16[1,128,384]{2,1,0:T(8,128)(2,1)S(1)} %copy-done.2, f32[1,384]{1,0:T(1,128)S(1)} %copy-done.5, s32[4,16]{1,0:T(4,128)S(1)} %copy-done.4), custom_call_target="tpu_custom_call" | custom-call | tf_op jit(solution)/shard_map/variances/pallas_call | solution.py:343
  72.2 0.6 copy.8
Async XLA Ops:
  0.0 0.9 %copy-start = (bf16[2,128,512]{2,1,0:T(8,128)(2,1)S(1)}, bf16[2,128,512]{2,1,0:T(8,128)(2,1)}, u32[]{:S(2)}) copy-start(bf16[2,128,512]{2,1,0:T(8,128)(2,1)} %f_ref.1) | copy-start | bytes 786436
  1.0 0.9 %copy-start.1 = (bf16[2,64,512]{2,1,0:T(8,128)(2,1)S(1)}, bf16[2,64,512]{2,1,0:T(8,128)(2,1)}, u32[]{:S(2)}) copy-start(bf16[2,64,512]{2,1,0:T(8,128)(2,1)} %l_ref.1) | copy-start | bytes 393220
  1.9 0.9 %copy-start.2 = (bf16[1,128,384]{2,1,0:T(8,128)(2,1)S(1)}, bf16[1,128,384]{2,1,0:T(8,128)(2,1)}, u32[]{:S(2)}) copy-start(bf16[1,128,384]{2,1,0:T(8,128)(2,1)} %v_ref.1) | copy-start | bytes 294916
  2.7 0.8 %copy-start.3 = (bf16[128,256]{1,0:T(8,128)(2,1)S(1)}, bf16[128,256]{1,0:T(8,128)(2,1)}, u32[]{:S(2)}) copy-start(bf16[128,256]{1,0:T(8,128)(2,1)} %r_ref.1) | copy-start | bytes 196612
  3.6 0.7 copy-start.4
  4.3 0.7 copy-start.5

commit v2 on v1

v2 whole, which is shorter than its diff:
```python
import jax
import jax.numpy as jnp
from jax import lax
from jax.experimental import pallas as pl
from jax.experimental.pallas import tpu as pltpu
from jax.sharding import PartitionSpec as P

NX, NU, NZ = 4, 4, 8
BLK = 128
SUB = 96
SLOTS = 16
MESH = pl.DeviceIdType.MESH
BF16, F32 = jnp.bfloat16, jnp.float32
NT = (((1,), (1,)), ((), ()))


def dot_nt(a, b):
    return lax.dot_general(a, b, NT, preferred_element_type=F32)


def kernel(
    r_hbm, f_hbm, l_hbm, v_hbm, loc_hbm, map_hbm, out_ref,
    r_in, f_in, l_in, v_in, loc_in, map_in,
    vs, vall, fg, lg, rg, wk, wm, acc, zacc, sums, l_acc, red,
    in_sem, vsc_s, vsc_r, vz_s, vz_r, fy_s, fy_r, fx_s, fx_r, fd_s, fd_r,
    ly_s, ly_r, lx_s, lx_r, ld_s, ld_r, ry_s, ry_r, rx_s, rx_r, rd_s, rd_r,
    wc_s, wc_r, wf_s, wf_r, wz_s, wz_r, red_s, red_r,
):
    leaf, x, col = lax.axis_index("leaf"), lax.axis_index("row"), lax.axis_index("col")
    h, c = lax.div(leaf, 2), lax.rem(leaf, 2)
    u, z = lax.div(col, NZ), lax.rem(col, NZ)
    y = h * NU + u
    sgn = 1 - 2 * c

    def at_z(zz):
        return (leaf, x, u * NZ + zz)

    def at_u(uu):
        return (leaf, x, uu * NZ + z)

    def at_x(xx):
        return (leaf, xx, col)

    def at_y(yy, core):
        return (lax.div(yy, NU) * 2 + core, x, lax.rem(yy, NU) * NZ + z)

    def zmod(v):
        return lax.rem(v + 2 * NZ, NZ)

    def xmod(v):
        return lax.rem(v + 2 * NX, NX)

    def umod(v):
        return lax.rem(v + 2 * NU, NU)

    started = []

    def send(src, dst, ssem, rsem, to):
        copy = pltpu.make_async_remote_copy(
            src_ref=src, dst_ref=dst, send_sem=ssem, recv_sem=rsem, device_id=to, device_id_type=MESH
        )
        copy.start()
        started.append(copy)

    def settle():
        while started:
            started.pop(0).wait_send()

    def arrived(dst, rsem):
        pltpu.make_async_remote_copy(
            src_ref=dst, dst_ref=dst, send_sem=rsem, recv_sem=rsem, device_id=at_z(zmod(z + 1)), device_id_type=MESH
        ).wait_recv()

    barrier = pltpu.get_barrier_semaphore()
    peers = []
    for d in range(1, 16):
        number = lax.rem(y * 2 + c + d, 16)
        peers.append(at_y(lax.div(number, 2), lax.rem(number, 2)))
    peers += [at_z(zmod(z + d)) for d in (1, 2, 6, 7)]
    peers += [at_x(xmod(x + 1)), at_x(xmod(x - 1))]
    v_copy = pltpu.make_async_copy(v_hbm.at[0], v_in, in_sem.at[0])
    v_copy.start()
    for peer in peers:
        pl.semaphore_signal(barrier, inc=1, device_id=peer, device_id_type=MESH)

    half = pl.ds(pl.multiple_of(c * 64, 64), 64)
    quarter = pl.ds(pl.multiple_of(c * 32, 32), 32)
    loads = [
        pltpu.make_async_copy(f_hbm.at[:, half], f_in, in_sem.at[1]),
        pltpu.make_async_copy(f_hbm.at[h, half], fg.at[x, u, c], in_sem.at[2]),
        pltpu.make_async_copy(r_hbm, r_in, in_sem.at[3]),
        pltpu.make_async_copy(l_hbm.at[:, quarter], l_in, in_sem.at[4]),
        pltpu.make_async_copy(l_hbm.at[h, quarter], lg.at[x, u, c], in_sem.at[5]),
        pltpu.make_async_copy(loc_hbm, loc_in, in_sem.at[6]),
        pltpu.make_async_copy(map_hbm, map_in, in_sem.at[7]),
    ]
    for copy in loads:
        copy.start()
    v_copy.wait()
    vs[...] = jnp.transpose(v_in[...].astype(F32)).astype(BF16).reshape(NU, SUB, BLK)
    for copy in loads:
        copy.wait()
    pl.semaphore_wait(barrier, len(peers))

    pltpu.make_async_copy(vs.at[u], vall.at[z, u], vsc_r.at[u]).start()
    for d in range(1, NU):
        to = umod(u + d)
        send(vs.at[to], vall.at[z, u], vsc_s.at[d], vsc_r.at[u], at_u(to))
    xa, xb, xo = xmod(x + sgn), xmod(x - sgn), xmod(x + 2)
    y_steps = [sgn, -sgn, 2 * sgn]
    for i, step in enumerate(y_steps):
        yy = lax.rem(y + step + 16, 8)
        send(f_in.at[lax.div(yy, NU)], fg.at[x, u, c], fy_s.at[i], fy_r.at[i], at_y(yy, c))
    u_from = [u] + [umod(u - step) for step in y_steps]

    def f_x_first(i):
        if i > 0:
            arrived(fg.at[x, u_from[i], c], fy_r.at[i - 1])
        send(fg.at[x, u_from[i], c], fg.at[x, u_from[i], c], fx_s.at[i, 0], fx_r.at[i, 0], at_x(xa))
        send(fg.at[x, u_from[i], c], fg.at[x, u_from[i], c], fx_s.at[i, 1], fx_r.at[i, 1], at_x(xb))

    def f_x_second(i):
        arrived(fg.at[xb, u_from[i], c], fx_r.at[i, 0])
        send(fg.at[xb, u_from[i], c], fg.at[xb, u_from[i], c], fx_s.at[i, 2], fx_r.at[i, 2], at_x(xa))

    def z_first(array, part, ssem, rsem, way):
        block = array.at[z, part]
        send(block, block, ssem.at[2], rsem.at[2], at_z(zmod(z + 2 * way)))
        send(block, block, ssem.at[1], rsem.at[1], at_z(zmod(z + way)))

    def z_second(array, part, ssem, rsem, way, last):
        block = array.at[zmod(z - 2 * way), part]
        arrived(block, rsem.at[2])
        if last == 4:
            send(block, block, ssem.at[4], rsem.at[4], at_z(zmod(z + 2 * way)))
        send(block, block, ssem.at[3], rsem.at[3], at_z(zmod(z + way)))

    def z_last(array, part, rsem, way, numbers):
        for number in numbers:
            arrived(array.at[zmod(z - number * way), part], rsem.at[number])

    upper, lower = pl.ds(2, 2), pl.ds(0, 2)

    def v_first(part, number):
        z_first(vall, part, vz_s.at[number], vz_r.at[number], sgn)
        z_first(vall, part, vz_s.at[number + 1], vz_r.at[number + 1], -sgn)

    def v_second(part, number):
        z_second(vall, part, vz_s.at[number], vz_r.at[number], sgn, 4)
        z_second(vall, part, vz_s.at[number + 1], vz_r.at[number + 1], -sgn, 3)

    def v_last(part, number):
        z_last(vall, part, vz_r.at[number], sgn, (1, 3, 4))
        z_last(vall, part, vz_r.at[number + 1], -sgn, (1, 3))

    sibling = (h * 2 + 1 - c, x, col)

    def to_sibling(array, xx, i, ssem, rsem):
        send(array.at[xx, :, c], array.at[xx, :, c], ssem.at[i], rsem.at[i], sibling)

    def from_sibling(array, rsem, places):
        for i, xx in enumerate(places):
            arrived(array.at[xx, :, 1 - c], rsem.at[i])

    def bulk_x_first(array, ssem, rsem):
        send(array.at[x, :, c], array.at[x, :, c], ssem.at[0], rsem.at[0], at_x(xa))
        send(array.at[x, :, c], array.at[x, :, c], ssem.at[1], rsem.at[1], at_x(xb))

    def bulk_x_second(array, ssem, rsem):
        arrived(array.at[xb, :, c], rsem.at[0])
        send(array.at[xb, :, c], array.at[xb, :, c], ssem.at[2], rsem.at[2], at_x(xa))

    f_x_first(0)
    arrived(vall.at[z, 2], vsc_r.at[2])
    arrived(vall.at[z, 3], vsc_r.at[3])
    v_first(upper, 0)
    f_x_first(1)
    f_x_first(2)
    arrived(vall.at[z, 0], vsc_r.at[0])
    arrived(vall.at[z, 1], vsc_r.at[1])
    v_first(lower, 2)
    f_x_second(0)
    f_x_first(3)
    to_sibling(fg, x, 0, fd_s, fd_r)
    target = leaf
    r_sends = []
    for t in range(2):
        for core in range(2):
            rows = r_in.at[pl.ds(core * 64, 64)]
            place = rg.at[x, u, core]
            mine = jnp.logical_and(jnp.logical_and(h == t, c == core), u == target)
            copy = pltpu.make_async_remote_copy(
                src_ref=rows, dst_ref=place, send_sem=ry_s.at[t * 2 + core], recv_sem=ry_r.at[u],
                device_id=(2 * t + core, x, target * NZ + z), device_id_type=MESH,
            )
            r_sends.append((mine, copy))

            @pl.when(mine)
            def _():
                pltpu.make_async_copy(rows, place, ry_r.at[u]).start()

            @pl.when(jnp.logical_not(mine))
            def _():
                copy.start()
    v_second(upper, 0)
    f_x_second(1)
    f_x_second(2)
    v_second(lower, 2)
    for i, step in enumerate(y_steps):
        yy = lax.rem(y + step + 16, 8)
        send(l_in.at[lax.div(yy, NU)], lg.at[x, u, c], ly_s.at[i], ly_r.at[i], at_y(yy, c))
    f_x_second(3)
    to_sibling(fg, xb, 1, fd_s, fd_r)
    for i in range(4):
        arrived(fg.at[xa, u_from[i], c], fx_r.at[i, 1])
    to_sibling(fg, xa, 2, fd_s, fd_r)
    for i in range(4):
        block = fg.at[xo, u_from[i], c]
        arrived(block, fx_r.at[i, 2])
        send(block, block, fd_s.at[3 + i], fd_r.at[3 + i], sibling)
    for i in range(4):
        arrived(rg.at[x, i, c], ry_r.at[i])
    bulk_x_first(rg, rx_s, rx_r)
    for i in range(1, 4):
        arrived(lg.at[x, u_from[i], c], ly_r.at[i - 1])
    bulk_x_first(lg, lx_s, lx_r)
    v_last(upper, 0)
    from_sibling(fg, fd_r, (x, xa, xb))
    for i, uu in enumerate([u] + [umod(u + step) for step in y_steps]):
        arrived(fg.at[xo, uu, 1 - c], fd_r.at[3 + i])

    def p_chunk(xx):
        return jnp.concatenate([vall[4 * (xx % 2) + i, 2 + xx // 2] for i in range(4)], axis=1)

    for pair in range(2):
        total = jnp.zeros((SUB, 256), F32)
        for xx in range(NX):
            total += dot_nt(p_chunk(xx), fg[xx, 2 * pair:2 * pair + 2].reshape(256, 512))
        acc[pair] = total
    v_last(lower, 2)
    for b in range(NU):
        block = b * NZ + z
        slot = jnp.int32(0)
        present = jnp.int32(0)
        for k in range(SLOTS):
            hit = map_in[leaf, k] == block
            slot = jnp.where(hit, k, slot)
            present = jnp.where(hit, 1, present)
        padded = vall[lax.rem(slot, NZ), lax.div(slot, NZ)].astype(F32) * present.astype(F32)
        wm[u, b] = (padded - acc[b // 2, :, (b % 2) * BLK:(b % 2 + 1) * BLK]).astype(BF16)

    pltpu.make_async_copy(wm.at[u, u], wk.at[z, u], wc_r.at[0]).start()
    for d in range(1, NU):
        to = umod(u + d)
        send(wm.at[u, to], wk.at[z, u], wc_s.at[d], wc_r.at[d], at_u(to))
    order = (0, 1, 3, 2)
    parts = [pl.ds(umod(u - d), 1) for d in order]
    for k in range(NU):
        arrived(wk.at[z, parts[k]], wc_r.at[order[k]])
        z_first(wk, parts[k], wz_s.at[k], wz_r.at[k], -sgn)
        if k == 0:
            for d in range(1, NU):
                to = umod(u + d)
                send(wm.at[u], wm.at[u], wf_s.at[d], wf_r.at[d], at_u(to))
    for array, xs, xr, ds, dr in ((rg, rx_s, rx_r, rd_s, rd_r), (lg, lx_s, lx_r, ld_s, ld_r)):
        bulk_x_second(array, xs, xr)
        to_sibling(array, x, 0, ds, dr)
        to_sibling(array, xb, 1, ds, dr)
        arrived(array.at[xa, :, c], xr.at[1])
        to_sibling(array, xa, 2, ds, dr)
    for k in range(NU):
        z_second(wk, parts[k], wz_s.at[k], wz_r.at[k], -sgn, 4)
    for array, xr, ds, dr in ((rg, rx_r, rd_s, rd_r), (lg, lx_r, ld_s, ld_r)):
        arrived(array.at[xo, :, c], xr.at[2])
        to_sibling(array, xo, 3, ds, dr)

    from_sibling(lg, ld_r, (x, xa, xb, xo))
    total = jnp.zeros((SUB, 256), F32)
    for xx in range(NX):
        total += dot_nt(p_chunk(xx), lg[xx].reshape(256, 512))
    lane = lax.broadcasted_iota(jnp.int32, (SUB, BLK), 1)
    odd = lax.rem(z, 2).astype(F32)
    l_sum = jnp.zeros((SUB, BLK), F32)
    for pair in range(2):
        one, two = (vall[4 * i + lax.div(z, 2), 2 + pair].astype(F32) for i in range(2))
        one_turned, two_turned = pltpu.roll(one, 64, 1), pltpu.roll(two, 64, 1)
        rows = jnp.where(
            lane < 64, one_turned * odd + one * (1.0 - odd), two * odd + two_turned * (1.0 - odd)
        )
        l_sum += rows * total[:, pair * BLK:(pair + 1) * BLK]
    l_acc[...] = l_sum
    from_sibling(rg, rd_r, (x, xa, xb, xo))
    settle()

    def w_rows(d):
        block = wk[zmod(z + sgn * d)].reshape(NU * SUB, BLK)
        return block * 2 if 1 <= d <= 3 else block

    def r_block(pair, d):
        zz = zmod(z + sgn * d)
        lanes = pl.ds(pl.multiple_of(lax.rem(zz, 2) * BLK, BLK), BLK)
        return rg[lax.div(zz, 2), 2 * pair:2 * pair + 2, :, :, lanes].reshape(256, BLK)

    for k in range(NU):
        z_last(wk, parts[k], wz_r.at[k], -sgn, (1, 3))
    left = jnp.concatenate([w_rows(d) for d in range(4)], axis=1)
    for pair in range(2):
        zacc[pair] = dot_nt(left, jnp.concatenate([r_block(pair, d) for d in range(4)], axis=1))
    for d in range(1, NU):
        arrived(wm.at[umod(u - d)], wf_r.at[d])
    for k in range(NU):
        z_last(wk, parts[k], wz_r.at[k], -sgn, (4,))
    part = jnp.zeros((NU * SUB, BLK), F32)
    for pair in range(2):
        term = zacc[pair] + dot_nt(w_rows(4), r_block(pair, 4))
        for i in range(2):
            rows = wm[:, 2 * pair + i].reshape(NU * SUB, BLK).astype(F32)
            part += rows * term[:, i * BLK:(i + 1) * BLK]
    sums[...] = part
    own_rows = pl.ds(pl.multiple_of(u * SUB, SUB), SUB)
    sums[own_rows, :] = sums[own_rows, :] + l_acc[...]
    flat = jnp.sum(jnp.transpose(sums[...]), axis=0, keepdims=True)
    red[z, u] = jnp.concatenate(
        [flat[:, i * BLK:(i + 1) * BLK] for i in range(3)] + [jnp.zeros((5, BLK), F32)], axis=0
    )
    pairs = [(dz, du) for du in (2, 3, 1, 0) for dz in (4, 3, 5, 2, 6, 1, 7, 0) if dz or du]
    for i, (dz, du) in enumerate(pairs):
        to = (leaf, x, umod(u + du) * NZ + zmod(z + dz))
        send(red.at[z, u], red.at[z, u], red_s.at[i], red_r.at[i], to)
    for i, (dz, du) in enumerate(pairs):
        arrived(red.at[zmod(z - dz), umod(u - du)], red_r.at[i])
    result = jnp.sum(red[...].reshape(NZ * NU, 8, BLK), axis=0)
    out_ref[...] = loc_in[...] + jnp.concatenate([result[i:i + 1] for i in range(3)], axis=1)

    settle()
    for mine, copy in r_sends:
        @pl.when(jnp.logical_not(mine))
        def _():
            copy.wait_send()


def local(root_inverse, factor_first, local_first, factor_second, local_second, ancestor_map):
    dma = pltpu.SemaphoreType.DMA
    scratch = [
        pltpu.VMEM(root_inverse.shape, BF16),
        pltpu.VMEM((2, 64, 512), BF16),
        pltpu.VMEM((2, 32, 512), BF16),
        pltpu.VMEM(factor_second.shape[1:], BF16),
        pltpu.VMEM(local_second.shape, F32),
        pltpu.SMEM(ancestor_map.shape, jnp.int32),
        pltpu.VMEM((NU, SUB, BLK), BF16),
        pltpu.VMEM((NZ, NU, SUB, BLK), BF16),
        pltpu.VMEM((NX, NU, 2, 64, 512), BF16),
        pltpu.VMEM((NX, NU, 2, 32, 512), BF16),
        pltpu.VMEM((NX, NU, 2, 64, 256), BF16),
        pltpu.VMEM((NZ, NU, SUB, BLK), BF16),
        pltpu.VMEM((NU, NU, SUB, BLK), BF16),
        pltpu.VMEM((2, SUB, 256), F32),
        pltpu.VMEM((2, NU * SUB, 256), F32),
        pltpu.VMEM((NU * SUB, BLK), F32),
        pltpu.VMEM((SUB, BLK), F32),
        pltpu.VMEM((NZ, NU, 8, BLK), F32),
        dma((8,)),
    ]
    for count in ((4,), (4, 5), (3,), (4, 3), (7,), (3,), (3,), (4,), (4,), (3,), (4,), (4,), (4,), (4, 5), (31,)):
        scratch += [dma(count), dma(count)]
    return pl.pallas_call(
        kernel,
        out_shape=jax.ShapeDtypeStruct(local_second.shape, F32),
        in_specs=[pl.BlockSpec(memory_space=pltpu.HBM)] * 6,
        out_specs=pl.BlockSpec(memory_space=pltpu.VMEM),
        scratch_shapes=scratch,
        compiler_params=pltpu.CompilerParams(
            collective_id=0, has_side_effects=True, vmem_limit_bytes=65_000_000
        ),
        name="variances",
    )(root_inverse, factor_first, local_first, factor_second, local_second, ancestor_map)


def solution(mesh):
    placed = (
        P("col", ("leaf", "row")),
        P(None, "col", "row"),
        P(None, "col", "row"),
        P("leaf", "col", "row"),
        P("leaf", "row"),
        P(),
    )
    return jax.shard_map(
        local, mesh=mesh, in_specs=placed, out_specs=P("leaf", "row"), check_vma=False
    )
```

time: 73 us -> 58.8 us (0.81)
  the two profiles are of different devices: /device:TPU:56 before, /device:TPU:1 now
where the time goes in v2:
time: 58.8 us; the launch traced here: 58.7 us
  Pallas kernels  57.4 us (98%)
  local copies, waits for them, and re-layouts  1.24 us (2%)
    pallas_call x1, Pallas kernels, local(): pl.pallas_call(kernel, out_shape=jax.ShapeDtypeStruct(local_second.shape,...  57.4 us
    unnamed x1, local copies, waits for them, and re-layouts  1.24 us

profile of v2, /device:TPU:1, one launch (start us, length us, event | category | flops | bytes accessed | tf_op | source)
XLA Modules:
  0.0 58.7 jit_solution(2731318364920075780)
XLA Ops:
  0.0 57.4 %variances.1 = f32[1,384]{1,0:T(1,128)} custom-call(bf16[128,256]{1,0:T(8,128)(2,1)} %r_hbm.1, bf16[2,128,512]{2,1,0:T(8,128)(2,1)} %f_hbm.1, bf16[2,64,512]{2,1,0:T(8,128)(2,1)} %l_hbm.1, bf16[1,128,384]{2,1,0:T(8,128)(2,1)} %v_hbm.1, f32[1,384]{1,0:T(1,128)} %loc_hbm.1, s32[4,16]{1,0:T(4,128)} %map_hbm.1), custom_call_target="tpu_custom_call" | custom-call | tf_op jit(solution)/shard_map/variances/pallas_call | solution.py:367
  57.4 1.2 %copy.8 = f32[1,384]{1,0:T(1,128)} copy(f32[1,384]{1,0:T(1,128)} %variances.1) | data formatting | bytes 3072

commit v3 on v2

--- a/solution.py
+++ b/solution.py
@@ -205,12 +205,12 @@
     v_second(upper, 0)
     f_x_second(1)
     f_x_second(2)
+    f_x_second(3)
+    to_sibling(fg, xb, 1, fd_s, fd_r)
     v_second(lower, 2)
     for i, step in enumerate(y_steps):
         yy = lax.rem(y + step + 16, 8)
         send(l_in.at[lax.div(yy, NU)], lg.at[x, u, c], ly_s.at[i], ly_r.at[i], at_y(yy, c))
-    f_x_second(3)
-    to_sibling(fg, xb, 1, fd_s, fd_r)
     for i in range(4):
         arrived(fg.at[xa, u_from[i], c], fx_r.at[i, 1])
     to_sibling(fg, xa, 2, fd_s, fd_r)
@@ -258,10 +258,13 @@
     for k in range(NU):
         arrived(wk.at[z, parts[k]], wc_r.at[order[k]])
         z_first(wk, parts[k], wz_s.at[k], wz_r.at[k], -sgn)
-        if k == 0:
-            for d in range(1, NU):
-                to = umod(u + d)
-                send(wm.at[u], wm.at[u], wf_s.at[d], wf_r.at[d], at_u(to))
+    for d in range(1, NU):
+        to = umod(u + d)
+        for i in range(1, NU):
+            rows = wm.at[u, umod(to + i)]
+            send(rows, rows, wf_s.at[d, i], wf_r.at[d, i], at_u(to))
+    for d in range(1, NU):
+        wm[umod(u - d), u] = wk[z, umod(u - d)]
     for array, xs, xr, ds, dr in ((rg, rx_s, rx_r, rd_s, rd_r), (lg, lx_s, lx_r, ld_s, ld_r)):
         bulk_x_second(array, xs, xr)
         to_sibling(array, x, 0, ds, dr)
@@ -307,7 +310,8 @@
     for pair in range(2):
         zacc[pair] = dot_nt(left, jnp.concatenate([r_block(pair, d) for d in range(4)], axis=1))
     for d in range(1, NU):
-        arrived(wm.at[umod(u - d)], wf_r.at[d])
+        for i in range(1, NU):
+            arrived(wm.at[umod(u - d), umod(u + i)], wf_r.at[d, i])
     for k in range(NU):
         z_last(wk, parts[k], wz_r.at[k], -sgn, (4,))
     part = jnp.zeros((NU * SUB, BLK), F32)
@@ -320,16 +324,17 @@
     own_rows = pl.ds(pl.multiple_of(u * SUB, SUB), SUB)
     sums[own_rows, :] = sums[own_rows, :] + l_acc[...]
     flat = jnp.sum(jnp.transpose(sums[...]), axis=0, keepdims=True)
-    red[z, u] = jnp.concatenate(
+    me = z * NU + u
+    red[me] = jnp.concatenate(
         [flat[:, i * BLK:(i + 1) * BLK] for i in range(3)] + [jnp.zeros((5, BLK), F32)], axis=0
     )
-    pairs = [(dz, du) for du in (2, 3, 1, 0) for dz in (4, 3, 5, 2, 6, 1, 7, 0) if dz or du]
-    for i, (dz, du) in enumerate(pairs):
-        to = (leaf, x, umod(u + du) * NZ + zmod(z + dz))
-        send(red.at[z, u], red.at[z, u], red_s.at[i], red_r.at[i], to)
-    for i, (dz, du) in enumerate(pairs):
-        arrived(red.at[zmod(z - dz), umod(u - du)], red_r.at[i])
-    result = jnp.sum(red[...].reshape(NZ * NU, 8, BLK), axis=0)
+    others = [i + (i >= me).astype(jnp.int32) for i in range(NZ * NU - 1)]
+    for i, other in enumerate(others):
+        to = (leaf, x, lax.rem(other, NU) * NZ + lax.div(other, NU))
+        send(red.at[me], red.at[me], red_s.at[i], red_r.at[me], to)
+    for other in others:
+        arrived(red.at[other], red_r.at[other])
+    result = jnp.sum(red[...], axis=0)
     out_ref[...] = loc_in[...] + jnp.concatenate([result[i:i + 1] for i in range(3)], axis=1)
 
     settle()
@@ -359,10 +364,10 @@
         pltpu.VMEM((2, NU * SUB, 256), F32),
         pltpu.VMEM((NU * SUB, BLK), F32),
         pltpu.VMEM((SUB, BLK), F32),
-        pltpu.VMEM((NZ, NU, 8, BLK), F32),
+        pltpu.VMEM((NZ * NU, 8, BLK), F32),
         dma((8,)),
     ]
-    for count in ((4,), (4, 5), (3,), (4, 3), (7,), (3,), (3,), (4,), (4,), (3,), (4,), (4,), (4,), (4, 5), (31,)):
+    for count in ((4,), (4, 5), (3,), (4, 3), (7,), (3,), (3,), (4,), (4,), (3,), (4,), (4,), (4, 4), (4, 5), (32,)):
         scratch += [dma(count), dma(count)]
     return pl.pallas_call(
         kernel,

time: 58.8 us -> 55.6 us (0.946)
  Pallas kernels: 57.4 us -> 54.2 us
    pallas_call x1, Pallas kernels: 57.4 us -> 54.2 us  [local(): pl.pallas_call(kernel, out_shape=jax.ShapeDtypeStruct(local_second.shape,...]
where the time goes in v3:
time: 55.6 us; the launch traced here: 55.4 us
  Pallas kernels  54.2 us (97%)
  local copies, waits for them, and re-layouts  1.24 us (2%)
    pallas_call x1, Pallas kernels, local(): pl.pallas_call(kernel, out_shape=jax.ShapeDtypeStruct(local_second.shape,...  54.2 us
    unnamed x1, local copies, waits for them, and re-layouts  1.24 us

profile of v3, /device:TPU:1, one launch (start us, length us, event | category | flops | bytes accessed | tf_op | source)
XLA Modules:
  0.0 55.4 jit_solution(3396356991108108952)
XLA Ops:
  0.0 54.2 %variances.1 = f32[1,384]{1,0:T(1,128)} custom-call(bf16[128,256]{1,0:T(8,128)(2,1)} %r_hbm.1, bf16[2,128,512]{2,1,0:T(8,128)(2,1)} %f_hbm.1, bf16[2,64,512]{2,1,0:T(8,128)(2,1)} %l_hbm.1, bf16[1,128,384]{2,1,0:T(8,128)(2,1)} %v_hbm.1, f32[1,384]{1,0:T(1,128)} %loc_hbm.1, s32[4,16]{1,0:T(4,128)} %map_hbm.1), custom_call_target="tpu_custom_call" | custom-call | tf_op jit(solution)/shard_map/variances/pallas_call | solution.py:372
  54.2 1.2 %copy.8 = f32[1,384]{1,0:T(1,128)} copy(f32[1,384]{1,0:T(1,128)} %variances.1) | data formatting | bytes 3072

commit v4 on v3

--- a/solution.py
+++ b/solution.py
@@ -72,16 +72,18 @@
         ).wait_recv()
 
     barrier = pltpu.get_barrier_semaphore()
-    peers = []
-    for d in range(1, 16):
-        number = lax.rem(y * 2 + c + d, 16)
-        peers.append(at_y(lax.div(number, 2), lax.rem(number, 2)))
-    peers += [at_z(zmod(z + d)) for d in (1, 2, 6, 7)]
-    peers += [at_x(xmod(x + 1)), at_x(xmod(x - 1))]
     v_copy = pltpu.make_async_copy(v_hbm.at[0], v_in, in_sem.at[0])
     v_copy.start()
+    peers = [at_y(lax.rem(y + d, 8), core) for d in (1, 2, 6, 7) for core in range(2)]
+    peers += [at_z(zmod(z + d)) for d in (1, 2, 6, 7)]
+    peers += [at_x(xmod(x + 1)), at_x(xmod(x - 1)), (h * 2 + 1 - c, x, col)]
     for peer in peers:
         pl.semaphore_signal(barrier, inc=1, device_id=peer, device_id_type=MESH)
+    outer = jnp.logical_or(u == 0, u == NU - 1)
+
+    @pl.when(outer)
+    def _():
+        pl.semaphore_signal(barrier, inc=1, device_id=at_u(NU - 1 - u), device_id_type=MESH)
 
     half = pl.ds(pl.multiple_of(c * 64, 64), 64)
     quarter = pl.ds(pl.multiple_of(c * 32, 32), 32)
@@ -98,14 +100,14 @@
         copy.start()
     v_copy.wait()
     vs[...] = jnp.transpose(v_in[...].astype(F32)).astype(BF16).reshape(NU, SUB, BLK)
+    vall[z, u] = vs[u]
+    pl.semaphore_wait(barrier, len(peers) + outer.astype(jnp.int32))
+
+    for d in range(1, NU):
+        to = umod(u + d)
+        send(vs.at[to], vall.at[z, u], vsc_s.at[d], vsc_r.at[d], at_u(to))
     for copy in loads:
         copy.wait()
-    pl.semaphore_wait(barrier, len(peers))
-
-    pltpu.make_async_copy(vs.at[u], vall.at[z, u], vsc_r.at[u]).start()
-    for d in range(1, NU):
-        to = umod(u + d)
-        send(vs.at[to], vall.at[z, u], vsc_s.at[d], vsc_r.at[u], at_u(to))
     xa, xb, xo = xmod(x + sgn), xmod(x - sgn), xmod(x + 2)
     y_steps = [sgn, -sgn, 2 * sgn]
     for i, step in enumerate(y_steps):
@@ -116,12 +118,15 @@
     def f_x_first(i):
         if i > 0:
             arrived(fg.at[x, u_from[i], c], fy_r.at[i - 1])
+        if i == 3:
+            send(fg.at[x, u_from[i], c], fg.at[x, u_from[i], c], fx_s.at[i, 2], fx_r.at[i, 2], at_x(xo))
         send(fg.at[x, u_from[i], c], fg.at[x, u_from[i], c], fx_s.at[i, 0], fx_r.at[i, 0], at_x(xa))
         send(fg.at[x, u_from[i], c], fg.at[x, u_from[i], c], fx_s.at[i, 1], fx_r.at[i, 1], at_x(xb))
 
     def f_x_second(i):
-        arrived(fg.at[xb, u_from[i], c], fx_r.at[i, 0])
-        send(fg.at[xb, u_from[i], c], fg.at[xb, u_from[i], c], fx_s.at[i, 2], fx_r.at[i, 2], at_x(xa))
+        if i != 3:
+            arrived(fg.at[xb, u_from[i], c], fx_r.at[i, 0])
+            send(fg.at[xb, u_from[i], c], fg.at[xb, u_from[i], c], fx_s.at[i, 2], fx_r.at[i, 2], at_x(xa))
 
     def z_first(array, part, ssem, rsem, way):
         block = array.at[z, part]
@@ -139,19 +144,22 @@
         for number in numbers:
             arrived(array.at[zmod(z - number * way), part], rsem.at[number])
 
-    upper, lower = pl.ds(2, 2), pl.ds(0, 2)
-
-    def v_first(part, number):
-        z_first(vall, part, vz_s.at[number], vz_r.at[number], sgn)
-        z_first(vall, part, vz_s.at[number + 1], vz_r.at[number + 1], -sgn)
-
-    def v_second(part, number):
-        z_second(vall, part, vz_s.at[number], vz_r.at[number], sgn, 4)
-        z_second(vall, part, vz_s.at[number + 1], vz_r.at[number + 1], -sgn, 3)
-
-    def v_last(part, number):
-        z_last(vall, part, vz_r.at[number], sgn, (1, 3, 4))
-        z_last(vall, part, vz_r.at[number + 1], -sgn, (1, 3))
+    v_parts = [pl.ds(umod(u - d), 1) for d in range(NU)]
+
+    def v_first(d):
+        if d:
+            arrived(vall.at[z, umod(u - d)], vsc_r.at[d])
+        for number, way in ((2 * d, sgn), (2 * d + 1, -sgn)):
+            z_first(vall, v_parts[d], vz_s.at[number], vz_r.at[number], way)
+
+    def v_second(d):
+        z_second(vall, v_parts[d], vz_s.at[2 * d], vz_r.at[2 * d], sgn, 4)
+        z_second(vall, v_parts[d], vz_s.at[2 * d + 1], vz_r.at[2 * d + 1], -sgn, 3)
+
+    def v_last():
+        for d in range(NU):
+            z_last(vall, v_parts[d], vz_r.at[2 * d], sgn, (1, 3, 4))
+            z_last(vall, v_parts[d], vz_r.at[2 * d + 1], -sgn, (1, 3))
 
     sibling = (h * 2 + 1 - c, x, col)
 
@@ -170,15 +178,14 @@
         arrived(array.at[xb, :, c], rsem.at[0])
         send(array.at[xb, :, c], array.at[xb, :, c], ssem.at[2], rsem.at[2], at_x(xa))
 
+    v_first(0)
     f_x_first(0)
-    arrived(vall.at[z, 2], vsc_r.at[2])
-    arrived(vall.at[z, 3], vsc_r.at[3])
-    v_first(upper, 0)
+    v_first(1)
+    v_first(3)
+    v_first(2)
     f_x_first(1)
     f_x_first(2)
-    arrived(vall.at[z, 0], vsc_r.at[0])
-    arrived(vall.at[z, 1], vsc_r.at[1])
-    v_first(lower, 2)
+    v_second(0)
     f_x_second(0)
     f_x_first(3)
     to_sibling(fg, x, 0, fd_s, fd_r)
@@ -202,15 +209,17 @@
             @pl.when(jnp.logical_not(mine))
             def _():
                 copy.start()
-    v_second(upper, 0)
-    f_x_second(1)
-    f_x_second(2)
-    f_x_second(3)
-    to_sibling(fg, xb, 1, fd_s, fd_r)
-    v_second(lower, 2)
     for i, step in enumerate(y_steps):
         yy = lax.rem(y + step + 16, 8)
         send(l_in.at[lax.div(yy, NU)], lg.at[x, u, c], ly_s.at[i], ly_r.at[i], at_y(yy, c))
+    v_second(1)
+    v_second(3)
+    f_x_second(1)
+    f_x_second(2)
+    v_second(2)
+    f_x_second(3)
+    arrived(fg.at[xb, u_from[3], c], fx_r.at[3, 0])
+    to_sibling(fg, xb, 1, fd_s, fd_r)
     for i in range(4):
         arrived(fg.at[xa, u_from[i], c], fx_r.at[i, 1])
     to_sibling(fg, xa, 2, fd_s, fd_r)
@@ -224,7 +233,7 @@
     for i in range(1, 4):
         arrived(lg.at[x, u_from[i], c], ly_r.at[i - 1])
     bulk_x_first(lg, lx_s, lx_r)
-    v_last(upper, 0)
+    v_last()
     from_sibling(fg, fd_r, (x, xa, xb))
     for i, uu in enumerate([u] + [umod(u + step) for step in y_steps]):
         arrived(fg.at[xo, uu, 1 - c], fd_r.at[3 + i])
@@ -237,7 +246,6 @@
         for xx in range(NX):
             total += dot_nt(p_chunk(xx), fg[xx, 2 * pair:2 * pair + 2].reshape(256, 512))
         acc[pair] = total
-    v_last(lower, 2)
     for b in range(NU):
         block = b * NZ + z
         slot = jnp.int32(0)
@@ -325,17 +333,14 @@
     sums[own_rows, :] = sums[own_rows, :] + l_acc[...]
     flat = jnp.sum(jnp.transpose(sums[...]), axis=0, keepdims=True)
     me = z * NU + u
-    red[me] = jnp.concatenate(
-        [flat[:, i * BLK:(i + 1) * BLK] for i in range(3)] + [jnp.zeros((5, BLK), F32)], axis=0
-    )
+    red[me] = flat
     others = [i + (i >= me).astype(jnp.int32) for i in range(NZ * NU - 1)]
     for i, other in enumerate(others):
         to = (leaf, x, lax.rem(other, NU) * NZ + lax.div(other, NU))
         send(red.at[me], red.at[me], red_s.at[i], red_r.at[me], to)
     for other in others:
         arrived(red.at[other], red_r.at[other])
-    result = jnp.sum(red[...], axis=0)
-    out_ref[...] = loc_in[...] + jnp.concatenate([result[i:i + 1] for i in range(3)], axis=1)
+    out_ref[...] = loc_in[...] + jnp.sum(red[...], axis=0)
 
     settle()
     for mine, copy in r_sends:
@@ -364,10 +369,10 @@
         pltpu.VMEM((2, NU * SUB, 256), F32),
         pltpu.VMEM((NU * SUB, BLK), F32),
         pltpu.VMEM((SUB, BLK), F32),
-        pltpu.VMEM((NZ * NU, 8, BLK), F32),
+        pltpu.VMEM((NZ * NU, 1, NU * SUB), F32),
         dma((8,)),
     ]
-    for count in ((4,), (4, 5), (3,), (4, 3), (7,), (3,), (3,), (4,), (4,), (3,), (4,), (4,), (4, 4), (4, 5), (32,)):
+    for count in ((4,), (8, 5), (3,), (4, 3), (7,), (3,), (3,), (4,), (4,), (3,), (4,), (4,), (4, 4), (4, 5), (32,)):
         scratch += [dma(count), dma(count)]
     return pl.pallas_call(
         kernel,

time: 55.6 us -> 54 us (0.971)
  Pallas kernels: 54.2 us -> 52.6 us
    pallas_call x1, Pallas kernels: 54.2 us -> 52.6 us  [local(): pl.pallas_call(kernel, out_shape=jax.ShapeDtypeStruct(local_second.shape,...]
where the time goes in v4:
time: 54 us; the launch traced here: 53.9 us
  Pallas kernels  52.6 us (97%)
  local copies, waits for them, and re-layouts  1.24 us (2%)
    pallas_call x1, Pallas kernels, local(): pl.pallas_call(kernel, out_shape=jax.ShapeDtypeStruct(local_second.shape,...  52.6 us
    unnamed x1, local copies, waits for them, and re-layouts  1.24 us

profile of v4, /device:TPU:1, one launch (start us, length us, event | category | flops | bytes accessed | tf_op | source)
XLA Modules:
  0.0 53.9 jit_solution(12319546246840558556)
XLA Ops:
  0.0 52.6 %variances.1 = f32[1,384]{1,0:T(1,128)} custom-call(bf16[128,256]{1,0:T(8,128)(2,1)} %r_hbm.1, bf16[2,128,512]{2,1,0:T(8,128)(2,1)} %f_hbm.1, bf16[2,64,512]{2,1,0:T(8,128)(2,1)} %l_hbm.1, bf16[1,128,384]{2,1,0:T(8,128)(2,1)} %v_hbm.1, f32[1,384]{1,0:T(1,128)} %loc_hbm.1, s32[4,16]{1,0:T(4,128)} %map_hbm.1), custom_call_target="tpu_custom_call" | custom-call | tf_op jit(solution)/shard_map/variances/pallas_call | solution.py:377
  52.6 1.2 %copy.8 = f32[1,384]{1,0:T(1,128)} copy(f32[1,384]{1,0:T(1,128)} %variances.1) | data formatting | bytes 3072

commit v5 on v4

--- a/solution.py
+++ b/solution.py
@@ -320,17 +320,21 @@
     for d in range(1, NU):
         for i in range(1, NU):
             arrived(wm.at[umod(u - d), umod(u + i)], wf_r.at[d, i])
+    def by_rows(terms):
+        part = jnp.zeros((NU * SUB, BLK), F32)
+        for pair in range(2):
+            term = terms(pair)
+            for i in range(2):
+                rows = wm[:, 2 * pair + i].reshape(NU * SUB, BLK).astype(F32)
+                part += rows * term[:, i * BLK:(i + 1) * BLK]
+        return part
+
+    sums[...] = by_rows(lambda pair: zacc[pair])
+    own_rows = pl.ds(pl.multiple_of(u * SUB, SUB), SUB)
+    sums[own_rows, :] = sums[own_rows, :] + l_acc[...]
     for k in range(NU):
         z_last(wk, parts[k], wz_r.at[k], -sgn, (4,))
-    part = jnp.zeros((NU * SUB, BLK), F32)
-    for pair in range(2):
-        term = zacc[pair] + dot_nt(w_rows(4), r_block(pair, 4))
-        for i in range(2):
-            rows = wm[:, 2 * pair + i].reshape(NU * SUB, BLK).astype(F32)
-            part += rows * term[:, i * BLK:(i + 1) * BLK]
-    sums[...] = part
-    own_rows = pl.ds(pl.multiple_of(u * SUB, SUB), SUB)
-    sums[own_rows, :] = sums[own_rows, :] + l_acc[...]
+    sums[...] = sums[...] + by_rows(lambda pair: dot_nt(w_rows(4), r_block(pair, 4)))
     flat = jnp.sum(jnp.transpose(sums[...]), axis=0, keepdims=True)
     me = z * NU + u
     red[me] = flat

time: 54 us -> 54.2 us (level)
  no operation moved by 1% of the time
where the time goes in v5:
time: 54.2 us; the launch traced here: 54 us
  Pallas kernels  52.7 us (97%)
  local copies, waits for them, and re-layouts  1.24 us (2%)
    pallas_call x1, Pallas kernels, local(): pl.pallas_call(kernel, out_shape=jax.ShapeDtypeStruct(local_second.shape,...  52.7 us
    unnamed x1, local copies, waits for them, and re-layouts  1.24 us

profile of v5, /device:TPU:1, one launch (start us, length us, event | category | flops | bytes accessed | tf_op | source)
XLA Modules:
  0.0 54.0 jit_solution(13310642643227407502)
XLA Ops:
  0.0 52.7 %variances.1 = f32[1,384]{1,0:T(1,128)} custom-call(bf16[128,256]{1,0:T(8,128)(2,1)} %r_hbm.1, bf16[2,128,512]{2,1,0:T(8,128)(2,1)} %f_hbm.1, bf16[2,64,512]{2,1,0:T(8,128)(2,1)} %l_hbm.1, bf16[1,128,384]{2,1,0:T(8,128)(2,1)} %v_hbm.1, f32[1,384]{1,0:T(1,128)} %loc_hbm.1, s32[4,16]{1,0:T(4,128)} %map_hbm.1), custom_call_target="tpu_custom_call" | custom-call | tf_op jit(solution)/shard_map/variances/pallas_call | solution.py:381
  52.8 1.2 %copy.8 = f32[1,384]{1,0:T(1,128)} copy(f32[1,384]{1,0:T(1,128)} %variances.1) | data formatting | bytes 3072

commit v6 on v5

--- a/solution.py
+++ b/solution.py
@@ -136,9 +136,9 @@
     def z_second(array, part, ssem, rsem, way, last):
         block = array.at[zmod(z - 2 * way), part]
         arrived(block, rsem.at[2])
+        send(block, block, ssem.at[3], rsem.at[3], at_z(zmod(z + way)))
         if last == 4:
             send(block, block, ssem.at[4], rsem.at[4], at_z(zmod(z + 2 * way)))
-        send(block, block, ssem.at[3], rsem.at[3], at_z(zmod(z + way)))
 
     def z_last(array, part, rsem, way, numbers):
         for number in numbers:

time: 54.2 us -> 53.9 us (level)
  no operation moved by 1% of the time
where the time goes in v6:
time: 53.9 us; the launch traced here: 53.8 us
  Pallas kernels  52.5 us (97%)
  local copies, waits for them, and re-layouts  1.24 us (2%)
    pallas_call x1, Pallas kernels, local(): pl.pallas_call(kernel, out_shape=jax.ShapeDtypeStruct(local_second.shape,...  52.5 us
    unnamed x1, local copies, waits for them, and re-layouts  1.24 us

profile of v6, /device:TPU:1, one launch (start us, length us, event | category | flops | bytes accessed | tf_op | source)
XLA Modules:
  0.0 53.8 jit_solution(11070433292685515680)
XLA Ops:
  0.0 52.5 %variances.1 = f32[1,384]{1,0:T(1,128)} custom-call(bf16[128,256]{1,0:T(8,128)(2,1)} %r_hbm.1, bf16[2,128,512]{2,1,0:T(8,128)(2,1)} %f_hbm.1, bf16[2,64,512]{2,1,0:T(8,128)(2,1)} %l_hbm.1, bf16[1,128,384]{2,1,0:T(8,128)(2,1)} %v_hbm.1, f32[1,384]{1,0:T(1,128)} %loc_hbm.1, s32[4,16]{1,0:T(4,128)} %map_hbm.1), custom_call_target="tpu_custom_call" | custom-call | tf_op jit(solution)/shard_map/variances/pallas_call | solution.py:381
  52.5 1.2 %copy.8 = f32[1,384]{1,0:T(1,128)} copy(f32[1,384]{1,0:T(1,128)} %variances.1) | data formatting | bytes 3072
